TPU v7x, 128 devices: a whole 4x4x4 slice. The times are simulated.
128 devices in a mesh: grp: 4 (over z), shard: 32 (over x, y, core).
Axes of the slice: x: 4, y: 4, z: 4, core: 2. Of those that a mesh axis runs over, the one named last changes fastest.
Arguments:
- queries: bfloat16 [256, 4, 128, 128], P(('grp', 'shard')), may hold values from -40 to 40
- prefix_keys: bfloat16 [16, 32, 1024, 128], P('grp', 'shard'), may hold values from -6 to 6
- prefix_values: bfloat16 [16, 32, 1024, 128], P('grp', 'shard'), may hold values from -6 to 6
- suffix_keys: bfloat16 [256, 512, 8, 128], P(('grp', 'shard')), may hold values from -6 to 6
- suffix_values: bfloat16 [256, 512, 8, 128], P(('grp', 'shard')), may hold values from -6 to 6
- new_keys: bfloat16 [256, 4, 8, 128], P(('grp', 'shard')), may hold values from -6 to 6
- new_values: bfloat16 [256, 4, 8, 128], P(('grp', 'shard')), may hold values from -6 to 6
- suffix_lengths: int32 [256], P(('grp', 'shard')), may hold values from 64 to 512
- branch_prefix: int32 [256], P(('grp', 'shard')), may hold values from 0 to 15, as said below
- prefix_slot: int32 [16], replicated, may hold values from 0 to 15, as said below
Outputs:
- attended: bfloat16 [256, 4, 128, 128], P(('grp', 'shard'))
Inputs may be any that keep to these rules, and one draw needn't show every extreme that they name: `branch_prefix`: slot s lies on group s // 4. Among the 2 branches of one device (aligned blocks of 2), at most 1 have prefixes whose slots lie in one group, and in every block some group has exactly 1. `prefix_slot`: each prefix has a slot of its own.
All inputs are finite; a program needn't handle non-finite values.
Results may differ from a plain program's by a relative error of at most 0.0056.
Values may be sent and summed in bfloat16 or wider, within the bound.
A program may use at most 64 MiB of HBM per device.

v0:
```python
import math

import jax
import jax.numpy as jnp
from jax import lax
from jax.sharding import PartitionSpec as P


def batch_attend(batch_item, keys_local, values_local, score_scale):
    query_rows, slot_pick = batch_item
    slot_count = keys_local.shape[0]
    result_out = None
    result_lse = None
    for slot_number in range(slot_count):
        scores = (
            jnp.einsum(
                "nrd,id->nri",
                query_rows,
                keys_local[slot_number],
                preferred_element_type=jnp.float32,
            )
            * score_scale
        )
        block_max = jnp.max(scores, axis=2)
        weight = jnp.exp(scores - block_max[:, :, None])
        block_total = jnp.sum(weight, axis=2)
        mixture = jnp.einsum(
            "nri,id->nrd",
            weight.astype(jnp.bfloat16),
            values_local[slot_number],
            preferred_element_type=jnp.float32,
        )
        slot_out = (mixture / block_total[:, :, None]).astype(jnp.bfloat16)
        slot_lse = block_max + jnp.log(block_total)
        if result_out is None:
            result_out = slot_out
            result_lse = slot_lse
        else:
            is_hit = slot_pick == slot_number
            result_out = jnp.where(is_hit[:, None, None], slot_out, result_out)
            result_lse = jnp.where(is_hit[:, None], slot_lse, result_lse)
    return (result_out, result_lse)


def holder_work(received, keys_local, values_local, score_scale):
    query_buffer, index_buffer = received
    senders, per_sender, row_count, head_width = query_buffer.shape
    item_count = senders * per_sender
    batch_width = math.gcd(item_count, 16)
    turns = item_count // batch_width
    flat_queries = query_buffer.reshape(turns, batch_width, row_count, head_width)
    flat_index = index_buffer.reshape(turns, batch_width).astype(jnp.int32)

    def attend_batch(batch_item):
        return batch_attend(batch_item, keys_local, values_local, score_scale)

    block_outs, block_lses = lax.map(attend_batch, (flat_queries, flat_index))
    return (
        block_outs.reshape(senders, per_sender, row_count, head_width),
        block_lses.reshape(senders, per_sender, row_count),
    )


def body(
    queries,
    prefix_keys,
    prefix_values,
    suffix_keys,
    suffix_values,
    new_keys,
    new_values,
    suffix_lengths,
    branch_prefix,
    prefix_slot,
):
    groups = lax.axis_size("grp")
    shards = lax.axis_size("shard")
    branches, step_count, head_count, head_width = queries.shape
    kv_heads = suffix_keys.shape[2]
    per_kv = head_count // kv_heads
    blocks = shards // kv_heads
    per_group = prefix_keys.shape[0]
    capacity = max(branches // 2, 1)
    score_scale = 1.0 / math.sqrt(head_width)
    row_count = step_count * per_kv
    keys_local = prefix_keys[:, 0]
    values_local = prefix_values[:, 0]
    slot_of = prefix_slot[branch_prefix]
    dest_group = slot_of // per_group
    local_slot = slot_of % per_group
    branch_order = jnp.arange(branches, dtype=jnp.int32)
    earlier_same = (dest_group[:, None] == dest_group[None, :]) & (
        branch_order[:, None] > branch_order[None, :]
    )
    position_in = jnp.sum(earlier_same.astype(jnp.int32), axis=1)
    placement = (
        dest_group[None, None, :] == jnp.arange(groups, dtype=jnp.int32)[:, None, None]
    ) & (position_in[None, None, :] == jnp.arange(capacity, dtype=jnp.int32)[None, :, None])
    placement_bf = placement.astype(jnp.bfloat16)
    slot_index = jnp.sum(placement.astype(jnp.int32) * local_slot[None, None, :], axis=2).astype(
        jnp.bfloat16
    )
    split_queries = queries.reshape(branches, step_count, kv_heads, per_kv, head_width)
    packed = jnp.einsum(
        "gcb,btkhd->gkcthd", placement_bf, split_queries, preferred_element_type=jnp.float32
    ).astype(jnp.bfloat16)
    spread = jnp.broadcast_to(
        packed[:, None], (groups, blocks, kv_heads, capacity, step_count, per_kv, head_width)
    ).reshape(groups * shards, capacity, row_count, head_width)
    index_spread = jnp.broadcast_to(
        slot_index[:, None, None, :], (groups, blocks, kv_heads, capacity)
    ).reshape(groups * shards, capacity)
    block_outs, block_lses = holder_work(
        (
            lax.all_to_all(spread, ("grp", "shard"), split_axis=0, concat_axis=0, tiled=True),
            lax.all_to_all(index_spread, ("grp", "shard"), split_axis=0, concat_axis=0, tiled=True),
        ),
        keys_local,
        values_local,
        score_scale,
    )
    back_out = lax.all_to_all(
        block_outs.astype(jnp.float32), ("grp", "shard"), split_axis=0, concat_axis=0, tiled=True
    ).astype(block_outs.dtype)
    back_lse = lax.all_to_all(block_lses, ("grp", "shard"), split_axis=0, concat_axis=0, tiled=True)
    back_out = back_out.reshape(groups, blocks, kv_heads, capacity, step_count, per_kv, head_width)
    back_lse = back_lse.reshape(groups, blocks, kv_heads, capacity, step_count, per_kv)
    prefix_out = back_out[dest_group, :, :, position_in].astype(jnp.float32)
    prefix_lse = back_lse[dest_group, :, :, position_in]
    scores_own = (
        jnp.einsum(
            "btkhd,bskd->bkths", split_queries, suffix_keys, preferred_element_type=jnp.float32
        )
        * score_scale
    )
    suffix_position = jnp.arange(suffix_keys.shape[1], dtype=jnp.int32)
    scores_own = jnp.where(
        suffix_position[None, None, None, None, :] < suffix_lengths[:, None, None, None, None],
        scores_own,
        -jnp.inf,
    )
    scores_new = (
        jnp.einsum("btkhd,bukd->bkthu", split_queries, new_keys, preferred_element_type=jnp.float32)
        * score_scale
    )
    step_position = jnp.arange(step_count, dtype=jnp.int32)
    causal = step_position[None, :] <= step_position[:, None]
    scores_new = jnp.where(causal[None, None, :, None, :], scores_new, -jnp.inf)
    own_max = jnp.maximum(jnp.max(scores_own, axis=-1), jnp.max(scores_new, axis=-1))
    weight_own = jnp.exp(scores_own - own_max[..., None])
    weight_new = jnp.exp(scores_new - own_max[..., None])
    own_total = jnp.sum(weight_own, axis=-1) + jnp.sum(weight_new, axis=-1)
    own_mix = jnp.einsum(
        "bkths,bskd->bkthd",
        weight_own.astype(jnp.bfloat16),
        suffix_values,
        preferred_element_type=jnp.float32,
    )
    own_mix = own_mix + jnp.einsum(
        "bkthu,bukd->bkthd",
        weight_new.astype(jnp.bfloat16),
        new_values,
        preferred_element_type=jnp.float32,
    )
    own_out = own_mix / own_total[..., None]
    own_lse = own_max + jnp.log(own_total)
    ceiling_all = jnp.maximum(jnp.max(prefix_lse, axis=1), own_lse)
    prefix_factor = jnp.exp(prefix_lse - ceiling_all[:, None])
    own_factor = jnp.exp(own_lse - ceiling_all)
    numerator = (
        jnp.sum(prefix_factor[..., None] * prefix_out, axis=1) + own_factor[..., None] * own_out
    )
    denominator = jnp.sum(prefix_factor, axis=1) + own_factor
    result = numerator / denominator[..., None]
    return (
        result.transpose(0, 2, 1, 3, 4)
        .reshape(branches, step_count, head_count, head_width)
        .astype(jnp.bfloat16)
    )


def solution(mesh):
    in_specs = (
        P(("grp", "shard"), None, None, None),
        P("grp", "shard", None, None),
        P("grp", "shard", None, None),
        P(("grp", "shard"), None, None, None),
        P(("grp", "shard"), None, None, None),
        P(("grp", "shard"), None, None, None),
        P(("grp", "shard"), None, None, None),
        P(("grp", "shard")),
        P(("grp", "shard")),
        P(),
    )
    out_specs = P(("grp", "shard"), None, None, None)
    return jax.shard_map(body, mesh=mesh, in_specs=in_specs, out_specs=out_specs, check_vma=False)
```

profile of v0, /device:TPU:1, one launch (start us, length us, event | category | flops | bytes accessed | tf_op | source)
XLA Modules:
  0.0 245.3 jit_solution(17096380810733037222)
XLA Ops:
  3.2 11.5 %all-to-all-start = ((bf16[128,1,1]{2,1,0:T(2,128)(2,1)}), bf16[128,1,1]{2,1,0:T(2,128)(2,1)S(1)}, u32[]{:S(2)}, u32[]{:S(2)}) async-start(bf16[128,1,1]{2,1,0:T(2,128)(2,1)} %broadcast_in_dim.143), calls=%async_computation | async-start | bytes 131072 | tf_op jit(solution)/shard_map/all_to_all | solution.py:116
  17.0 7.2 %all-to-all-done = bf16[128,1,1]{2,1,0:T(2,128)(2,1)S(1)} async-done(((bf16[128,1,1]{2,1,0:T(2,128)(2,1)}), bf16[128,1,1]{2,1,0:T(2,128)(2,1)S(1)}, u32[]{:S(2)}, u32[]{:S(2)}) %all-to-all-start) | async-done | bytes 288 | tf_op jit(solution)/shard_map/all_to_all | solution.py:116
  24.3 2.9 %broadcast_in_dim.137 = bf16[4,4,8,4,16,128]{5,4,3,2,1,0:T(8,128)(2,1)} broadcast(bf16[4,8,4,16,128]{4,3,2,1,0:T(8,128)(2,1)} %copy.55), dimensions={0,2,3,4,5} | broadcast | bytes 2621440 | tf_op jit(solution)/shard_map/broadcast_in_dim | solution.py:107
  27.2 5.3 %all-to-all-start.1 = ((bf16[128,1,64,128]{3,2,1,0:T(8,128)(2,1)}), bf16[128,1,64,128]{3,2,1,0:T(8,128)(2,1)}, u32[]{:S(2)}, u32[]{:S(2)}) async-start(bf16[128,1,64,128]{3,2,1,0:T(8,128)(2,1)} %bitcast.196), calls=%async_computation.1 | async-start | bytes 4194304 | tf_op jit(solution)/shard_map/all_to_all | solution.py:115
  32.5 2.4 convert_reduce_fusion
  34.9 27.8 %all-to-all-done.1 = bf16[128,1,64,128]{3,2,1,0:T(8,128)(2,1)} async-done(((bf16[128,1,64,128]{3,2,1,0:T(8,128)(2,1)}), bf16[128,1,64,128]{3,2,1,0:T(8,128)(2,1)}, u32[]{:S(2)}, u32[]{:S(2)}) %all-to-all-start.1) | async-done | bytes 2097184 | tf_op jit(solution)/shard_map/all_to_all | solution.py:115
  62.8 125.5 %while.12 = (s32[]{:T(128)}, bf16[8,16,64,128]{3,2,1,0:T(8,128)(2,1)}, f32[8,16,64]{2,1,0:T(8,128)}, s32[8,16]{1,0:T(8,128)S(1)}, bf16[8,16,64,128]{3,2,1,0:T(8,...) while((s32[]{:T(128)}, bf16[8,16,64,128]{3,2,1,0:T(8,128)(2,1)}, ...), condition=%wide.region_11.12_spmd, body=%wide.region_2.11_spmd.sunk | while | flops 2182478848 | bytes 59664180 | solution.py:57
  62.8 1.8 multiply_reduce_fusion.9
  66.3 1.8 fusion.193
  71.6 1.7 multiply_reduce_fusion.12
  73.4 1.8 fusion.196
  82.0 1.8 fusion.193
  87.3 1.7 multiply_reduce_fusion.12
  89.1 1.8 fusion.196
  97.7 1.8 fusion.193
  104.8 1.8 fusion.196
  113.3 1.8 fusion.193
  120.4 1.8 fusion.196
  129.0 1.8 fusion.193
  136.1 1.8 fusion.196
  144.7 1.8 fusion.193
  151.8 1.8 fusion.196
  160.4 1.8 fusion.193
  167.5 1.8 fusion.196
  176.1 1.8 fusion.193
  183.2 1.8 fusion.196
  188.3 4.4 %all-to-all-start.2 = ((f32[128,1,64]{2,1,0:T(1,128)}), f32[128,1,64]{2,1,0:T(1,128)S(1)}, u32[]{:S(2)}, u32[]{:S(2)}) async-start(f32[128,1,64]{2,1,0:T(1,128)} %bitcast.36), calls=%async_computation.2 | async-start | bytes 131072 | tf_op jit(solution)/shard_map/all_to_all | solution.py:125
  193.5 8.9 %all-to-all-done.2 = f32[128,1,64]{2,1,0:T(1,128)S(1)} async-done(((f32[128,1,64]{2,1,0:T(1,128)}), f32[128,1,64]{2,1,0:T(1,128)S(1)}, u32[]{:S(2)}, u32[]{:S(2)}) %all-to-all-start.2) | async-done | bytes 32800 | tf_op jit(solution)/shard_map/all_to_all | solution.py:125
  202.4 5.4 %all-to-all-start.3 = ((bf16[128,1,64,128]{3,2,1,0:T(8,128)(2,1)}), bf16[128,1,64,128]{3,2,1,0:T(8,128)(2,1)}, u32[]{:S(2)}, u32[]{:S(2)}) async-start(bf16[128,1,64,128]{3,2,1,0:T(8,128)(2,1)} %bitcast.197), calls=%async_computation.3 | async-start | bytes 4194304 | tf_op jit(solution)/shard_map/all_to_all | solution.py:122
  213.3 24.7 %all-to-all-done.3 = bf16[128,1,64,128]{3,2,1,0:T(8,128)(2,1)} async-done(((bf16[128,1,64,128]{3,2,1,0:T(8,128)(2,1)}), bf16[128,1,64,128]{3,2,1,0:T(8,128)(2,1)}, u32[]{:S(2)}, u32[]{:S(2)}) %all-to-all-start.3) | async-done | bytes 2097184 | tf_op jit(solution)/shard_map/all_to_all | solution.py:122
  238.1 2.3 gather_fusion.2
  241.2 3.4 %fusion.136 = bf16[2,4,8,16,128]{4,3,1,2,0:T(8,128)(2,1)S(1)} fusion(f32[2,8,4,16,128]{4,3,2,1,0:T(8,128)} %fusion.146, bf16[2,512,8,128,1]{3,2,1,0,4:T(8,128)(2,1)} %bitcast.207, f32[2,8,4,16,512]{4,3,2,1,0:T(8,128)} %copy-done.2, f32[2,8,4,16]{3,2,1,0:T(4,128)S(1)} %max.40, pred[2,512]{1,0:T(4,128)(4,1)S(1)} %iota_compare_fusion, ...), kind=kOutput, calls=%fused_computation.112 | convolution fusion | flops 137101312 | bytes 5522432 | tf_op jit(solution)/shard_map/bkths,bskd->bkthd/dot_general | solution.py:153
  (141 shorter events, 103.6 us)
Async XLA Ops:
  0.0 207.9 %copy-start = (bf16[2,512,8,128]{3,2,1,0:T(8,128)(2,1)S(1)}, bf16[2,512,8,128]{3,2,1,0:T(8,128)(2,1)}, u32[]{:S(2)}) copy-start(bf16[2,512,8,128]{3,2,1,0:T(8,128)(2,1)} %param.15) | copy-start | bytes 6291460
  3.2 21.0 %all-to-all-start = ((bf16[128,1,1]{2,1,0:T(2,128)(2,1)}), bf16[128,1,1]{2,1,0:T(2,128)(2,1)S(1)}, u32[]{:S(2)}, u32[]{:S(2)}) async-start(bf16[128,1,1]{2,1,0:T(2,128)(2,1)} %broadcast_in_dim.143), calls=%async_computation | async-start | bytes 131072 | tf_op jit(solution)/shard_map/all_to_all | solution.py:116
  16.1 46.6 %copy-start.1 = (bf16[4,1,1024,128]{3,2,1,0:T(8,128)(2,1)S(1)}, bf16[4,1,1024,128]{3,2,1,0:T(8,128)(2,1)}, u32[]{:S(2)}) copy-start(bf16[4,1,1024,128]{3,2,1,0:T(8,128)(2,1)} %param.13) | copy-start | bytes 3145732
  27.2 35.6 %all-to-all-start.1 = ((bf16[128,1,64,128]{3,2,1,0:T(8,128)(2,1)}), bf16[128,1,64,128]{3,2,1,0:T(8,128)(2,1)}, u32[]{:S(2)}, u32[]{:S(2)}) async-start(bf16[128,1,64,128]{3,2,1,0:T(8,128)(2,1)} %bitcast.196), calls=%async_computation.1 | async-start | bytes 4194304 | tf_op jit(solution)/shard_map/all_to_all | solution.py:115
  62.8 129.9 %copy-start.3 = (bf16[2,4,128,128]{3,2,1,0:T(8,128)(2,1)S(1)}, bf16[2,4,128,128]{3,2,1,0:T(8,128)(2,1)}, u32[]{:S(2)}) copy-start(bf16[2,4,128,128]{3,2,1,0:T(8,128)(2,1)} %param.12) | copy-start | bytes 786436
  62.8 129.9 %copy-start.7 = (bf16[2,4,8,128]{3,2,1,0:T(8,128)(2,1)S(1)}, bf16[2,4,8,128]{3,2,1,0:T(8,128)(2,1)}, u32[]{:S(2)}) copy-start(bf16[2,4,8,128]{3,2,1,0:T(8,128)(2,1)} %param.17) | copy-start | bytes 49156
  66.3 1.9 copy-start.6
  82.0 1.9 copy-start.6
  97.6 1.9 copy-start.6
  113.3 1.9 copy-start.6
  129.0 1.9 copy-start.6
  144.7 1.9 copy-start.6
  160.4 1.9 copy-start.6
  176.0 1.9 copy-start.6
  188.2 19.5 %copy-start.5 = (s32[2]{0:T(128)S(1)}, s32[2]{0:T(128)}, u32[]{:S(2)}) copy-start(s32[2]{0:T(128)} %param.19) | copy-start | bytes 28
  188.3 14.1 %all-to-all-start.2 = ((f32[128,1,64]{2,1,0:T(1,128)}), f32[128,1,64]{2,1,0:T(1,128)S(1)}, u32[]{:S(2)}, u32[]{:S(2)}) async-start(f32[128,1,64]{2,1,0:T(1,128)} %bitcast.36), calls=%async_computation.2 | async-start | bytes 131072 | tf_op jit(solution)/shard_map/all_to_all | solution.py:125
  202.4 6.7 %copy-start.4 = (bf16[2,4,8,128]{3,2,1,0:T(8,128)(2,1)S(1)}, bf16[2,4,8,128]{3,2,1,0:T(8,128)(2,1)}, u32[]{:S(2)}) copy-start(bf16[2,4,8,128]{3,2,1,0:T(8,128)(2,1)} %param.18) | copy-start | bytes 49156
  202.4 35.7 %all-to-all-start.3 = ((bf16[128,1,64,128]{3,2,1,0:T(8,128)(2,1)}), bf16[128,1,64,128]{3,2,1,0:T(8,128)(2,1)}, u32[]{:S(2)}, u32[]{:S(2)}) async-start(bf16[128,1,64,128]{3,2,1,0:T(8,128)(2,1)} %bitcast.197), calls=%async_computation.3 | async-start | bytes 4194304 | tf_op jit(solution)/shard_map/all_to_all | solution.py:122
  208.8 1.5 copy-start.2
where the time goes:
time: 247 us; the launch traced here: 245 us
  matrix products  97.9 us (40%)
  waiting for transfers between devices  68.7 us (28%)
  other arithmetic  40.9 us (17%)
  starting transfers between devices  26.6 us (11%)
  local copies, waits for them, and re-layouts  10.4 us (4%)
    dot_general x32, matrix products, batch_attend(): jnp.einsum('nrd,id->nri', query_rows, keys_local[slot_number], preferred_...  55.6 us
    dot_general x32, matrix products, batch_attend(): jnp.einsum('nri,id->nrd', weight.astype(jnp.bfloat16), values_local[slot_...  34.4 us
    reduce_sum x16, other arithmetic, batch_attend(): block_total = jnp.sum(weight, axis=2)  29.4 us
    all_to_all x1, waiting for transfers between devices, body(): lax.all_to_all(spread, ('grp', 'shard'), split_axis=0, concat_axis=0, til...  27.8 us
    all_to_all x1, waiting for transfers between devices, body(): lax.all_to_all(block_outs.astype(jnp.float32), ('grp', 'shard'), split_ax...  24.7 us
    all_to_all x1, starting transfers between devices, body(): lax.all_to_all(index_spread, ('grp', 'shard'), split_axis=0, concat_axis=...  11.5 us
    all_to_all x1, waiting for transfers between devices, body(): lax.all_to_all(block_lses, ('grp', 'shard'), split_axis=0, concat_axis=0,...  8.89 us
    all_to_all x1, waiting for transfers between devices, body(): lax.all_to_all(index_spread, ('grp', 'shard'), split_axis=0, concat_axis=...  7.23 us
  transfers between devices with their start and end apart: 4, of which 4 were waited for; matrix products, arithmetic and copies ran while one was open for 4% of the time, Pallas kernels for 0%

commit v1 on v0

v1 whole, which is shorter than its diff:
```python
import functools
import math

import jax
import jax.numpy as jnp
from jax import lax
from jax.experimental import pallas as pl
from jax.experimental.pallas import tpu as pltpu
from jax.sharding import PartitionSpec as P

MESH = pl.DeviceIdType.MESH
BF = jnp.bfloat16
F32 = jnp.float32
NT = (((1,), (1,)), ((), ()))
HD = 128
ROWS = 64
SLOTS = 32
TILES = 18
GROUP = 6
DZ_ORDER = (0, 1, 3, 2)
SCALE = math.log2(math.e) / math.sqrt(HD)


def coords():
    shard = lax.axis_index("shard")
    return lax.axis_index("grp"), shard // 8, (shard // 2) % 4, shard % 2


def place(index):
    return index // 8, (index // 2) % 4, index % 2


def at_offset(dz, dy, dc, sign=1):
    z, x, y, c = coords()
    shard = x * 8 + lax.rem(y + sign * dy + 4, 4) * 2 + lax.rem(c + dc, 2)
    return lax.rem(z + sign * dz + 4, 4), shard


def at_x(dx):
    z, x, y, c = coords()
    return z, lax.rem(x + dx + 4, 4) * 8 + y * 2 + c


def eye_mask(rows):
    shape = (rows, 128)
    return lax.broadcasted_iota(jnp.int32, shape, 0) == lax.broadcasted_iota(jnp.int32, shape, 1)


def to_row(column):
    return jnp.sum(jnp.where(eye_mask(column.shape[0]), column, 0.0), axis=0, keepdims=True)


def to_column(row):
    spread = jnp.where(eye_mask(ROWS), jnp.broadcast_to(row, (ROWS, 128)), 0.0)
    return jnp.sum(spread, axis=1, keepdims=True)


def merge(parts):
    top = functools.reduce(jnp.maximum, [lse for _, lse in parts])
    weights = [jnp.exp2(lse - top) for _, lse in parts]
    total = functools.reduce(jnp.add, weights)
    mixed = functools.reduce(jnp.add, [w * out for w, (out, _) in zip(weights, parts)])
    return mixed / total, top + jnp.log2(total)


def order_places(meta_ref, order_v, order_s, sem):
    column = meta_ref[...].reshape(SLOTS, 128)
    lane = lax.broadcasted_iota(jnp.int32, (SLOTS, 128), 1)
    line = lax.broadcasted_iota(jnp.int32, (SLOTS, 128), 0)
    row = jnp.sum(jnp.where(lane == line, column, 0), axis=0, keepdims=True)
    before = (column == row) & (lane < line)
    rank = jnp.sum(jnp.where(before, 1, 0), axis=1, keepdims=True)
    lane_row = lax.broadcasted_iota(jnp.int32, (1, 128), 1)
    start = jnp.zeros((1, 1), jnp.int32)
    position = rank
    tile_slot = jnp.zeros((1, 128), jnp.int32)
    for slot in range(4):
        position = position + jnp.where(column[:, :1] == slot, start, 0)
        count = jnp.sum(jnp.where((row == slot) & (lane_row < SLOTS), 1, 0), axis=1, keepdims=True)
        start = start + ((count + 1) & -2)
        if slot < 3:
            tile_slot = tile_slot + jnp.where(2 * lane_row >= start, 1, 0)
    position = jnp.broadcast_to(position, (SLOTS, 128))
    order_v[0:1] = jnp.sum(jnp.where(position == lane, line, 0), axis=0, keepdims=True)
    order_v[1:2] = jnp.sum(jnp.where(lane == line, position, 0), axis=0, keepdims=True)
    order_v[2:3] = tile_slot
    copy = pltpu.make_async_copy(order_v, order_s, sem)
    copy.start()
    copy.wait()


def read_order(order_s, line, index):
    return jnp.clip(order_s[line, index], 0, (SLOTS - 1, 2 * TILES - 1, 3)[line])


def attend_chunk(q_ref, order_s, keys_t, values_a, out_ref, lse_ref):
    def step(turn, carry):
        scores = []
        for unit in range(GROUP):
            tile = turn * GROUP + unit
            first = q_ref[read_order(order_s, 0, 2 * tile)]
            second = q_ref[read_order(order_s, 0, 2 * tile + 1)]
            rows = jnp.concatenate([first, second], axis=0)
            keys = keys_t[read_order(order_s, 2, tile)]
            scores.append(jnp.dot(rows, keys, preferred_element_type=F32))
        for unit in range(GROUP):
            tile = turn * GROUP + unit
            top = jnp.max(scores[unit], axis=1, keepdims=True)
            weight = jnp.exp2((scores[unit] - top) * SCALE).astype(BF)
            both = jnp.dot(weight, values_a[read_order(order_s, 2, tile)], preferred_element_type=F32)
            total = both[:, HD:]
            out = (both[:, :HD] / total).astype(BF)
            lse = top * SCALE + jnp.log2(total)
            out_ref[2 * tile] = out[:ROWS]
            out_ref[2 * tile + 1] = out[ROWS:]
            lse_ref[2 * tile] = lse[:ROWS]
            lse_ref[2 * tile + 1] = lse[ROWS:]
        return carry

    lax.fori_loop(0, TILES // GROUP, step, 0)


def spread_heads(src_ref, new_ref, branch, wide, wide_new):
    def step(turn, carry):
        part = src_ref[branch, pl.ds(turn * 64, 64)].astype(F32)
        wide[pl.ds(pl.multiple_of(turn * 512, 512), 512)] = part.reshape(512, HD)
        return carry

    lax.fori_loop(0, 8, step, 0)
    wide_new[0:32] = new_ref[branch].astype(F32).reshape(32, HD)


def own_branch(branch, b, length):
    sk, sv, nk, nv = b["sk_v"], b["sv_v"], b["nk_v"], b["nv_v"]
    spread_heads(sk, nk, branch, b["wide_k"], b["wide_nk"])
    spread_heads(sv, nv, branch, b["wide_v"], b["wide_nv"])
    pad = jnp.zeros((124, HD), F32)

    def step(turn, carry):
        pieces = []
        for unit in range(2):
            head = turn * 2 + unit
            keys = jnp.concatenate(
                [b["wide_k"][pl.ds(head, 512, stride=8)], b["wide_nk"][pl.ds(head, 4, stride=8)], pad], axis=0
            ).astype(BF)
            values = jnp.concatenate(
                [b["wide_v"][pl.ds(head, 512, stride=8)], b["wide_nv"][pl.ds(head, 4, stride=8)], pad], axis=0
            ).astype(BF)
            start = pl.multiple_of(head * 16, 16)
            rows = b["q_v"][branch, :, pl.ds(start, 16), :].reshape(ROWS, HD)
            scores = lax.dot_general(rows, keys, NT, preferred_element_type=F32)
            lane = lax.broadcasted_iota(jnp.int32, scores.shape, 1)
            stage = lax.broadcasted_iota(jnp.int32, scores.shape, 0) // 16
            live = (lane < length) | ((lane >= 512) & (lane - 512 <= stage))
            pieces.append((jnp.where(live, scores, -jnp.inf), values))
        for unit in range(2):
            head = turn * 2 + unit
            scores, values = pieces[unit]
            top = jnp.max(scores, axis=1, keepdims=True)
            weight = jnp.exp2((scores - top) * SCALE)
            total = jnp.sum(weight, axis=1, keepdims=True)
            mixed = jnp.dot(weight.astype(BF), values, preferred_element_type=F32)
            b["own_o"][branch, head] = mixed / total
            b["own_l"][branch, head] = jnp.broadcast_to(top * SCALE + jnp.log2(total), (ROWS, 128))
        return carry

    lax.fori_loop(0, 4, step, 0)


def pick_rows(order_s, out_ref, lse_ref, index):
    where = read_order(order_s, 1, index)
    return out_ref[where], lse_ref[where]


def kernel(prefix_ref, slot_ref, length_ref, q_hbm, pk_hbm, pv_hbm, sk_hbm, sv_hbm, nk_hbm, nv_hbm, o_ref, *scratch):
    b = dict(zip(NAMES, scratch))
    z, x, y, c = coords()

    def local(index, src, dst):
        copy = pltpu.make_async_copy(src, dst, b["local_sem"].at[index])
        copy.start()
        return copy

    load_q = local(0, q_hbm, b["q_v"])
    load_k = local(1, pk_hbm, b["pk_v"])
    load_v = local(2, pv_hbm, b["va"].at[:, :, pl.ds(0, HD)])
    load_own = [
        local(3, sk_hbm, b["sk_v"]),
        local(4, sv_hbm, b["sv_v"]),
        local(5, nk_hbm, b["nk_v"]),
        local(6, nv_hbm, b["nv_v"]),
    ]

    barrier = pltpu.get_barrier_semaphore()
    for index in range(1, SLOTS):
        pl.semaphore_signal(barrier, inc=1, device_id=at_offset(*place(index)), device_id_type=MESH)
    for dx in (1, -1):
        pl.semaphore_signal(barrier, inc=1, device_id=at_x(dx), device_id_type=MESH)

    slots = [slot_ref[prefix_ref[i]] for i in range(2)]
    groups = [s // 4 for s in slots]

    def remote(src, dst, send, recv, device):
        return pltpu.make_async_remote_copy(
            src_ref=src, dst_ref=dst, send_sem=send, recv_sem=recv, device_id=device, device_id_type=MESH
        )

    def q_copies(index):
        device = at_offset(*place(index))
        return (
            remote(b["sb"].at[index], b["qx0"].at[index], b["q_send"].at[index], b["q_recv"].at[index], device),
            remote(b["mb"].at[index // 8], b["mx0"].at[index], b["m_send"].at[index], b["m_recv"].at[index], device),
        )

    load_q.wait()
    started = False
    for dz in DZ_ORDER:
        group = lax.rem(z + dz, 4)
        second = (groups[1] == group).astype(jnp.int32)
        local_slot = jnp.where(groups[1] == group, slots[1], slots[0]) % 4
        b["mb"][dz] = jnp.full((1, 128), local_slot, jnp.int32)
        for low in range(8):
            index = dz * 8 + low
            _, dy, dc = place(index)
            head = lax.rem(y + dy, 4) * 2 + lax.rem(c + dc, 2)
            rows = b["q_v"][second, :, pl.ds(pl.multiple_of(head * 16, 16), 16), :].reshape(ROWS, HD)
            if index == 0:
                b["qx0"][0] = rows
                b["mx0"][0] = b["mb"][0]
            else:
                b["sb"][index] = rows
        if not started:
            pl.semaphore_wait(barrier, SLOTS - 1 + 2)
            started = True
        for low in range(8):
            index = dz * 8 + low
            if index:
                for copy in q_copies(index):
                    copy.start()

    def x_copies(dz, side):
        part = pl.ds(dz * 8, 8)
        target = b["qx1"] if side == 0 else b["qx2"]
        mtarget = b["mx1"] if side == 0 else b["mx2"]
        device = at_x(1 if side == 0 else -1)
        return (
            remote(b["qx0"].at[part], target.at[part], b["x_send"].at[side, dz], b["x_recv"].at[side, dz], device),
            remote(b["mx0"].at[part], mtarget.at[part], b["xm_send"].at[side, dz], b["xm_recv"].at[side, dz], device),
        )

    def f_copies(dz, side):
        part = pl.ds(dz * 8 + side * 4, 4)
        source = b["qx1"] if side == 0 else b["qx2"]
        msource = b["mx1"] if side == 0 else b["mx2"]
        device = at_x(1 if side == 0 else -1)
        return (
            remote(source.at[part], b["qx3"].at[part], b["f_send"].at[side, dz], b["f_recv"].at[side, dz], device),
            remote(msource.at[part], b["mx3"].at[part], b["fm_send"].at[side, dz], b["fm_recv"].at[side, dz], device),
        )

    def pass_x(dz):
        for low in range(8):
            index = dz * 8 + low
            if index:
                for copy in q_copies(index):
                    copy.wait_recv()
        for side in range(2):
            for copy in x_copies(dz, side):
                copy.start()

    def pass_on(dz):
        for side in range(2):
            for copy in x_copies(dz, side):
                copy.wait_recv()
            for copy in f_copies(dz, side):
                copy.start()

    for slot in range(4):
        b["va"][slot, :, HD:] = jnp.ones((1024, HD), BF)
    load_k.wait()
    for slot in range(4):
        b["kt"][slot] = b["pk_v"][slot].T
    pass_x(0)
    for copy in load_own:
        copy.wait()
    own_branch(0, b, length_ref[0])
    pass_x(1)
    pass_x(3)
    own_branch(1, b, length_ref[1])
    pass_x(2)
    load_v.wait()

    def chunk(number):
        order_places(b["mx%d" % number], b["order_v"], b["order%d" % number], b["local_sem"].at[7])
        attend_chunk(
            b["qx%d" % number], b["order%d" % number], b["kt"], b["va"], b["ot%d" % number], b["lt%d" % number]
        )

    def part_of(number, index):
        return pick_rows(b["order%d" % number], b["ot%d" % number], b["lt%d" % number], index)

    chunk(0)
    for dz in (0, 1, 3):
        pass_on(dz)
    pass_on(2)

    def a_copies(side):
        device = at_x(-1 if side == 0 else 1)
        return (
            remote(b["a_out"].at[side], b["a_in"].at[side], b["a_send"].at[side], b["a_recv"].at[side], device),
            remote(b["al_out"].at[side], b["al_in"].at[side], b["al_send"].at[side], b["al_recv"].at[side], device),
        )

    def c_copies(side, dz):
        device = at_x(-1 if side == 0 else 1)
        part = pl.ds(dz * 4, 4)
        lpart = pl.ds(dz * 8, 8)
        return (
            remote(
                b["c_out"].at[side, part], b["c_in"].at[side, part], b["c_send"].at[side, dz], b["c_recv"].at[side, dz], device
            ),
            remote(
                b["cl_out"].at[side, lpart], b["cl_in"].at[side, lpart], b["cl_send"].at[side, dz], b["cl_recv"].at[side, dz],
                device,
            ),
        )

    def b_copies(side, dz):
        device = at_x(-1 if side == 0 else 1)
        part = pl.ds(dz * 4, 4)
        lpart = pl.ds(dz * 8, 8)
        return (
            remote(
                b["b_out"].at[side, part], b["b_in"].at[side, part], b["b_send"].at[side, dz], b["b_recv"].at[side, dz], device
            ),
            remote(
                b["bl_out"].at[side, lpart], b["bl_in"].at[side, lpart], b["bl_send"].at[side, dz], b["bl_recv"].at[side, dz],
                device,
            ),
        )

    def send_plain(number, side, half, out, lse, dz_list, copies):
        for dz in dz_list:
            def step(low, carry):
                rows, column = part_of(number, dz * 8 + half * 4 + low)
                out[side, dz * 4 + low] = rows
                lse[side, pl.ds(dz * 8 + low, 1)] = to_row(column)
                return carry

            lax.fori_loop(0, 4, step, 0)
            for copy in copies(dz):
                copy.start()

    chunk(1)
    send_plain(1, 0, 1, b["a_out"], b["al_out"], range(4), lambda dz: a_copies(0) if dz == 3 else ())
    chunk(2)
    send_plain(2, 1, 0, b["a_out"], b["al_out"], range(4), lambda dz: a_copies(1) if dz == 3 else ())
    for dz in DZ_ORDER:
        for side in range(2):
            for copy in f_copies(dz, side):
                copy.wait_recv()
    chunk(3)
    for dz in DZ_ORDER:
        for side in range(2):
            send_plain(3, side, side, b["c_out"], b["cl_out"], [dz], functools.partial(c_copies, side))

    for dz in DZ_ORDER:
        for side in range(2):
            for copy in c_copies(side, dz):
                copy.wait_recv()

            def step(low, carry):
                rows, column = part_of(1 + side, dz * 8 + side * 4 + low)
                far = to_column(b["cl_in"][side, pl.ds(dz * 8 + low, 1)])
                out, lse = merge([(rows.astype(F32), column), (b["c_in"][side, dz * 4 + low].astype(F32), far)])
                b["b_out"][side, dz * 4 + low] = out.astype(BF)
                b["bl_out"][side, pl.ds(dz * 8 + low, 1)] = to_row(lse)
                return carry

            lax.fori_loop(0, 4, step, 0)
            for copy in b_copies(side, dz):
                copy.start()

    def h_copies(index):
        device = at_offset(*place(index), sign=-1)
        return (
            remote(b["h_out"].at[index], b["h_in"].at[index], b["h_send"].at[index], b["h_recv"].at[index], device),
            remote(b["hl_out"].at[index], b["hl_in"].at[index], b["hl_send"].at[index], b["hl_recv"].at[index], device),
        )

    for side in range(2):
        for copy in a_copies(side):
            copy.wait_recv()
    for dz in DZ_ORDER:
        for half in range(2):
            for copy in b_copies(half, dz):
                copy.wait_recv()

            def step(low, carry):
                index = dz * 8 + half * 4 + low
                rows, column = part_of(0, index)
                plain = to_column(b["al_in"][1 - half, pl.ds(dz * 8 + low, 1)])
                joined = to_column(b["bl_in"][half, pl.ds(dz * 8 + low, 1)])
                out, lse = merge(
                    [
                        (rows.astype(F32), column),
                        (b["a_in"][1 - half, dz * 4 + low].astype(F32), plain),
                        (b["b_in"][half, dz * 4 + low].astype(F32), joined),
                    ]
                )
                b["h_out"][index] = out.astype(BF)
                b["hl_out"][index] = to_row(lse)
                return carry

            lax.fori_loop(0, 4, step, 0)
            for low in range(4):
                index = dz * 8 + half * 4 + low
                if index:
                    for copy in h_copies(index):
                        copy.start()
                else:
                    b["h_in"][0] = b["h_out"][0]
                    b["hl_in"][0] = b["hl_out"][0]

    for index in range(1, SLOTS):
        for copy in h_copies(index):
            copy.wait_recv()

    for branch in range(2):
        away = lax.rem(groups[branch] - z + 4, 4)

        def step(low, carry):
            dy = low // 2
            dc = low % 2
            head = lax.rem(y + dy, 4) * 2 + lax.rem(c + dc, 2)
            from_prefix = b["h_in"][away * 8 + low].astype(F32)
            lse = to_column(b["hl_in"][away * 8 + low])
            out, _ = merge([(from_prefix, lse), (b["own_o"][branch, head], b["own_l"][branch, head])])
            o_ref[branch, :, pl.ds(pl.multiple_of(head * 16, 16), 16), :] = out.astype(BF).reshape(4, 16, HD)
            return carry

        lax.fori_loop(0, 8, step, 0)

    for index in range(1, SLOTS):
        for copy in q_copies(index) + h_copies(index):
            copy.wait_send()
    for side in range(2):
        for copy in a_copies(side):
            copy.wait_send()
        for dz in range(4):
            for copy in x_copies(dz, side) + f_copies(dz, side) + c_copies(side, dz) + b_copies(side, dz):
                copy.wait_send()


def scratch_shapes():
    dma = pltpu.SemaphoreType.DMA
    vmem = pltpu.VMEM
    shapes = {
        "q_v": vmem((2, 4, 128, HD), BF),
        "pk_v": vmem((4, 1024, HD), BF),
        "kt": vmem((4, HD, 1024), BF),
        "va": vmem((4, 1024, 2 * HD), BF),
        "sk_v": vmem((2, 512, 8, HD), BF),
        "sv_v": vmem((2, 512, 8, HD), BF),
        "nk_v": vmem((2, 4, 8, HD), BF),
        "nv_v": vmem((2, 4, 8, HD), BF),
        "wide_k": vmem((4104, HD), F32),
        "wide_v": vmem((4104, HD), F32),
        "wide_nk": vmem((40, HD), F32),
        "wide_nv": vmem((40, HD), F32),
        "own_o": vmem((2, 8, ROWS, HD), F32),
        "own_l": vmem((2, 8, ROWS, HD), F32),
        "sb": vmem((SLOTS, ROWS, HD), BF),
        "mb": vmem((4, 1, 128), jnp.int32),
        "order_v": vmem((8, 128), jnp.int32),
        "a_out": vmem((2, 16, ROWS, HD), BF),
        "a_in": vmem((2, 16, ROWS, HD), BF),
        "c_out": vmem((2, 16, ROWS, HD), BF),
        "c_in": vmem((2, 16, ROWS, HD), BF),
        "b_out": vmem((2, 16, ROWS, HD), BF),
        "b_in": vmem((2, 16, ROWS, HD), BF),
        "h_out": vmem((SLOTS, ROWS, HD), BF),
        "h_in": vmem((SLOTS, ROWS, HD), BF),
        "hl_out": vmem((SLOTS, 1, 128), F32),
        "hl_in": vmem((SLOTS, 1, 128), F32),
        "local_sem": dma((8,)),
    }
    for name in ("al", "cl", "bl"):
        shapes[name + "_out"] = vmem((2, 32, 128), F32)
        shapes[name + "_in"] = vmem((2, 32, 128), F32)
    for number in range(4):
        shapes["qx%d" % number] = vmem((SLOTS, ROWS, HD), BF)
        shapes["mx%d" % number] = vmem((SLOTS, 1, 128), jnp.int32)
        shapes["order%d" % number] = pltpu.SMEM((8, 128), jnp.int32)
        shapes["ot%d" % number] = vmem((2 * TILES, ROWS, HD), BF)
        shapes["lt%d" % number] = vmem((2 * TILES, ROWS, HD), F32)
    for name, count in (
        ("q", (SLOTS,)), ("m", (SLOTS,)), ("x", (2, 4)), ("xm", (2, 4)), ("f", (2, 4)), ("fm", (2, 4)),
        ("a", (2,)), ("al", (2,)), ("c", (2, 4)), ("cl", (2, 4)), ("b", (2, 4)), ("bl", (2, 4)),
        ("h", (SLOTS,)), ("hl", (SLOTS,)),
    ):
        shapes[name + "_send"] = dma(count)
        shapes[name + "_recv"] = dma(count)
    return shapes


NAMES = tuple(scratch_shapes())


def body(
    queries, prefix_keys, prefix_values, suffix_keys, suffix_values, new_keys, new_values, suffix_lengths, branch_prefix,
    prefix_slot,
):
    smem = pl.BlockSpec(memory_space=pltpu.SMEM)
    hbm = pl.BlockSpec(memory_space=pl.ANY)
    return pl.pallas_call(
        kernel,
        out_shape=jax.ShapeDtypeStruct(queries.shape, BF),
        in_specs=[smem] * 3 + [hbm] * 7,
        out_specs=pl.BlockSpec(memory_space=pltpu.VMEM),
        scratch_shapes=list(scratch_shapes().values()),
        compiler_params=pltpu.CompilerParams(collective_id=0, has_side_effects=True, vmem_limit_bytes=60 << 20),
        name="attend",
    )(
        branch_prefix, prefix_slot, suffix_lengths, queries, prefix_keys[:, 0], prefix_values[:, 0], suffix_keys,
        suffix_values, new_keys, new_values,
    )


def solution(mesh):
    both = P(("grp", "shard"), None, None, None)
    prefix = P("grp", "shard", None, None)
    flat = P(("grp", "shard"))
    return jax.shard_map(
        body,
        mesh=mesh,
        in_specs=(both, prefix, prefix, both, both, both, both, flat, flat, P()),
        out_specs=both,
        check_vma=False,
    )
```

time: 247 us -> 71.3 us (0.29)
  matrix products: 97.9 us -> 0 us
  Pallas kernels: 0 us -> 69.5 us
  waiting for transfers between devices: 68.7 us -> 0 us
  other arithmetic: 40.9 us -> 0 us
  starting transfers between devices: 26.6 us -> 0 us
  local copies, waits for them, and re-layouts: 10.4 us -> 1.67 us
    dot_general x69 -> x0, matrix products: 97.9 us -> none  [the longest x32 55.6 us: batch_attend(): jnp.einsum('nrd,id->nri', query_rows, keys_local[slot_number], preferred_...]
    pallas_call x0 -> x1, Pallas kernels: none -> 69.5 us  [body(): pl.pallas_call(kernel, out_shape=jax.ShapeDtypeStruct(queries.shape, BF),...]
    all_to_all x4 -> x0, waiting for transfers between devices: 68.7 us -> none  [the longest x1 27.8 us: body(): lax.all_to_all(spread, ('grp', 'shard'), split_axis=0, concat_axis=0, til...]
    reduce_sum x22 -> x0, other arithmetic: 31.2 us -> none  [the longest x16 29.4 us: batch_attend(): block_total = jnp.sum(weight, axis=2)]
    all_to_all x4 -> x0, starting transfers between devices: 26.6 us -> none  [the longest x1 11.5 us: body(): lax.all_to_all(index_spread, ('grp', 'shard'), split_axis=0, concat_axis=...]
    dynamic_update_slice x8 -> x0, other arithmetic: 5.38 us -> none  [holder_work(): block_outs, block_lses = lax.map(attend_batch, (flat_queries, flat_index))]
    broadcast_in_dim x4 -> x0, local copies, waits for them, and re-layouts: 4.62 us -> none  [the longest x2 3.82 us: body(): jnp.broadcast_to(packed[:, None], (groups, blocks, kv_heads, capacity, st...]
    gather x3 -> x0, local copies, waits for them, and re-layouts: 4.26 us -> none  [the longest x1 2.34 us: body(): prefix_out = back_out[dest_group, :, :, position_in].astype(jnp.float32)]
  transfers between devices with their start and end apart: 4 -> 0, of which waited for: 4 -> 0; matrix products, arithmetic and copies ran while one was open for 4% -> 0% of each run, Pallas kernels for 0% -> 0%
where the time goes in v1:
time: 71.3 us; the launch traced here: 71.2 us
  Pallas kernels  69.5 us (97%)
  local copies, waits for them, and re-layouts  1.67 us (2%)
    pallas_call x1, Pallas kernels, body(): pl.pallas_call(kernel, out_shape=jax.ShapeDtypeStruct(queries.shape, BF),...  69.5 us
    unnamed x1, local copies, waits for them, and re-layouts  1.67 us

profile of v1, /device:TPU:1, one launch (start us, length us, event | category | flops | bytes accessed | tf_op | source)
XLA Modules:
  0.0 71.2 jit_solution(12127914456546982151)
XLA Ops:
  0.0 69.5 %attend.1 = bf16[2,4,128,128]{3,2,1,0:T(8,128)(2,1)} custom-call(s32[2]{0:T(128)} %prefix_ref.1, s32[16]{0:T(128)} %slot_ref.1, s32[2]{0:T(128)} %length_ref.1, bf16[2,4,128,128]{3,2,1,0:T(8,128)(2,1)} %q_hbm.1, bf16[4,1024,128]{2,1,0:T(8,128)(2,1)} %bitcast.2, bf16[4,1024,128]{2,1,0:T(8,128)(2,1)} %bitcast.3, bf16[2,512,8,128]{3,2,1,0:T(8,128)(2,1)} %sk_hbm.1, ...), custom_call_target="tpu_custom_call" | custom-call | tf_op jit(solution)/shard_map/attend/pallas_call | solution.py:516
  69.5 1.7 %copy.12 = bf16[2,4,128,128]{3,2,1,0:T(8,128)(2,1)} copy(bf16[2,4,128,128]{3,2,1,0:T(8,128)(2,1)} %attend.1) | data formatting | bytes 524288

commit v2 on v1

v2 whole, which is shorter than its diff:
```python
import functools
import math

import jax
import jax.numpy as jnp
from jax import lax
from jax.experimental import pallas as pl
from jax.experimental.pallas import tpu as pltpu
from jax.sharding import PartitionSpec as P

MESH = pl.DeviceIdType.MESH
BF = jnp.bfloat16
F32 = jnp.float32
NT = (((1,), (1,)), ((), ()))
HD = 128
ROWS = 64
SLOTS = 32
TILES = 18
GROUP = 6
DZ_ORDER = (0, 1, 3, 2)
BACK_ORDER = (2, 1, 3, 0)
SCALE = math.log2(math.e) / math.sqrt(HD)


def beside(side, dz):
    return (1 if dz < 2 else 2), side * 16 + (8 if dz in (1, 2) else 0)


def coords():
    shard = lax.axis_index("shard")
    return lax.axis_index("grp"), shard // 8, (shard // 2) % 4, shard % 2


def place(index):
    return index // 8, (index // 2) % 4, index % 2


def at_offset(dz, dy, dc, sign=1):
    z, x, y, c = coords()
    shard = x * 8 + lax.rem(y + sign * dy + 4, 4) * 2 + lax.rem(c + dc, 2)
    return lax.rem(z + sign * dz + 4, 4), shard


def at_x(dx):
    z, x, y, c = coords()
    return z, lax.rem(x + dx + 4, 4) * 8 + y * 2 + c


def eye_mask(rows):
    shape = (rows, 128)
    return lax.broadcasted_iota(jnp.int32, shape, 0) == lax.broadcasted_iota(jnp.int32, shape, 1)


def to_row(column):
    return jnp.sum(jnp.where(eye_mask(column.shape[0]), column, 0.0), axis=0, keepdims=True)


def to_column(row):
    spread = jnp.where(eye_mask(ROWS), jnp.broadcast_to(row, (ROWS, 128)), 0.0)
    return jnp.sum(spread, axis=1, keepdims=True)


def merge(parts):
    top = functools.reduce(jnp.maximum, [lse for _, lse in parts])
    weights = [jnp.exp2(lse - top) for _, lse in parts]
    total = functools.reduce(jnp.add, weights)
    mixed = functools.reduce(jnp.add, [w * out for w, (out, _) in zip(weights, parts)])
    return mixed / total, top + jnp.log2(total)


def order_places(meta_refs, source_ref, order_v, order_s, sem):
    for low in range(8):
        for branch in range(2):
            row = 32 + 2 * low + branch
            order_v[row : row + 1] = source_ref[low, branch]
    lane = lax.broadcasted_iota(jnp.int32, (SLOTS, 128), 1)
    line = lax.broadcasted_iota(jnp.int32, (SLOTS, 128), 0)
    lane_row = lax.broadcasted_iota(jnp.int32, (1, 128), 1)
    for number, pieces in enumerate(meta_refs):
        column = jnp.concatenate([ref[dz].reshape(8, 128) for ref, dz in pieces], axis=0)
        row = jnp.sum(jnp.where(lane == line, column, 0), axis=0, keepdims=True)
        before = (column == row) & (lane < line)
        rank = jnp.sum(jnp.where(before, 1, 0), axis=1, keepdims=True)
        start = jnp.zeros((1, 1), jnp.int32)
        position = rank
        tile_slot = jnp.zeros((1, 128), jnp.int32)
        for slot in range(4):
            position = position + jnp.where(column[:, :1] == slot, start, 0)
            count = jnp.sum(jnp.where((row == slot) & (lane_row < SLOTS), 1, 0), axis=1, keepdims=True)
            start = start + ((count + 1) & -2)
            if slot < 3:
                tile_slot = tile_slot + jnp.where(2 * lane_row >= start, 1, 0)
        position = jnp.broadcast_to(position, (SLOTS, 128))
        order_v[8 * number : 8 * number + 1] = jnp.sum(jnp.where(position == lane, line, 0), axis=0, keepdims=True)
        order_v[8 * number + 1 : 8 * number + 2] = jnp.sum(
            jnp.where(lane == line, position, 0), axis=0, keepdims=True
        )
        order_v[8 * number + 2 : 8 * number + 3] = tile_slot
    copy = pltpu.make_async_copy(order_v, order_s, sem)
    copy.start()
    copy.wait()


def read_order(order, line, index):
    order_s, number = order
    return jnp.clip(order_s[8 * number + line, index], 0, (SLOTS - 1, 2 * TILES - 1, 3)[line])


def attend_chunk(q_ref, order_s, keys_t, values_a, out_ref, lse_ref):
    def step(turn, carry):
        scores = []
        for unit in range(GROUP):
            tile = turn * GROUP + unit
            first = q_ref[read_order(order_s, 0, 2 * tile)]
            second = q_ref[read_order(order_s, 0, 2 * tile + 1)]
            rows = jnp.concatenate([first, second], axis=0)
            keys = keys_t[read_order(order_s, 2, tile)]
            scores.append(jnp.dot(rows, keys, preferred_element_type=F32))
        for unit in range(GROUP):
            tile = turn * GROUP + unit
            top = jnp.max(scores[unit], axis=1, keepdims=True)
            weight = jnp.exp2((scores[unit] - top) * SCALE).astype(BF)
            both = jnp.dot(weight, values_a[read_order(order_s, 2, tile)], preferred_element_type=F32)
            total = both[:, HD:]
            out = (both[:, :HD] / total).astype(BF)
            lse = top * SCALE + jnp.log2(total)
            out_ref[2 * tile] = out[:ROWS]
            out_ref[2 * tile + 1] = out[ROWS:]
            lse_ref[2 * tile] = lse[:ROWS]
            lse_ref[2 * tile + 1] = lse[ROWS:]
        return carry

    lax.fori_loop(0, TILES // GROUP, step, 0)


def spread_heads(src_ref, new_ref, branch, wide, wide_new):
    def step(turn, carry):
        part = src_ref[branch, pl.ds(turn * 64, 64)].astype(F32)
        wide[pl.ds(pl.multiple_of(turn * 512, 512), 512)] = part.reshape(512, HD)
        return carry

    lax.fori_loop(0, 8, step, 0)
    wide_new[0:32] = new_ref[branch].astype(F32).reshape(32, HD)


def own_spread(branch, b):
    sk, sv, nk, nv = b["sk_v"], b["sv_v"], b["nk_v"], b["nv_v"]
    spread_heads(sk, nk, branch, b["wide_k"], b["wide_nk"])
    spread_heads(sv, nv, branch, b["wide_v"], b["wide_nv"])


def own_heads(branch, b, length, turns):
    pad = jnp.zeros((124, HD), F32)

    def step(turn, carry):
        pieces = []
        for unit in range(4):
            head = turn * 4 + unit
            keys = jnp.concatenate(
                [b["wide_k"][pl.ds(head, 512, stride=8)], b["wide_nk"][pl.ds(head, 4, stride=8)], pad], axis=0
            ).astype(BF)
            values = jnp.concatenate(
                [b["wide_v"][pl.ds(head, 512, stride=8)], b["wide_nv"][pl.ds(head, 4, stride=8)], pad], axis=0
            ).astype(BF)
            start = pl.multiple_of(head * 16, 16)
            rows = b["q_v"][branch, :, pl.ds(start, 16), :].reshape(ROWS, HD)
            scores = lax.dot_general(rows, keys, NT, preferred_element_type=F32)
            lane = lax.broadcasted_iota(jnp.int32, scores.shape, 1)
            stage = lax.broadcasted_iota(jnp.int32, scores.shape, 0) // 16
            live = (lane < length) | ((lane >= 512) & (lane - 512 <= stage))
            pieces.append((jnp.where(live, scores, -jnp.inf), values))
        for unit in range(4):
            head = turn * 4 + unit
            scores, values = pieces[unit]
            top = jnp.max(scores, axis=1, keepdims=True)
            weight = jnp.exp2((scores - top) * SCALE)
            total = jnp.sum(weight, axis=1, keepdims=True)
            mixed = jnp.dot(weight.astype(BF), values, preferred_element_type=F32)
            b["own_o"][branch, head] = mixed / total
            b["own_l"][branch, head] = jnp.broadcast_to(top * SCALE + jnp.log2(total), (ROWS, 128))
        return carry

    lax.fori_loop(*turns, step, 0)


def pick_rows(order_s, out_ref, lse_ref, index):
    where = read_order(order_s, 1, index)
    return out_ref[where], lse_ref[where]


def kernel(prefix_ref, slot_ref, length_ref, q_hbm, pk_hbm, pv_hbm, sk_hbm, sv_hbm, nk_hbm, nv_hbm, o_ref, *scratch):
    b = dict(zip(NAMES, scratch))
    z, x, y, c = coords()

    def local(index, src, dst):
        copy = pltpu.make_async_copy(src, dst, b["local_sem"].at[index])
        copy.start()
        return copy

    load_q = local(0, q_hbm, b["q_v"])
    load_k = local(1, pk_hbm, b["pk_v"])
    load_v = local(2, pv_hbm, b["va"].at[:, :, pl.ds(0, HD)])
    load_own = [
        local(3, sk_hbm, b["sk_v"]),
        local(4, sv_hbm, b["sv_v"]),
        local(5, nk_hbm, b["nk_v"]),
        local(6, nv_hbm, b["nv_v"]),
    ]

    barrier = pltpu.get_barrier_semaphore()
    partners = [at_offset(0, *place(low)[1:]) for low in range(1, 8)]
    partners += [at_offset(dz, 0, 0) for dz in range(1, 4)] + [at_x(1), at_x(-1)]
    for partner in partners:
        pl.semaphore_signal(barrier, inc=1, device_id=partner, device_id_type=MESH)

    slots = [slot_ref[prefix_ref[i]] for i in range(2)]
    groups = [s // 4 for s in slots]

    def remote(src, dst, send, recv, device):
        return pltpu.make_async_remote_copy(
            src_ref=src, dst_ref=dst, send_sem=send, recv_sem=recv, device_id=device, device_id_type=MESH
        )

    def pair(name, key, src, dst, device):
        return remote(src, dst, b[name + "_send"].at[key], b[name + "_recv"].at[key], device)

    def qy_copy(low):
        _, dy, dc = place(low)
        head = lax.rem(y + dy, 4) * 2 + lax.rem(c + dc, 2)
        rows = pl.ds(pl.multiple_of(head * 16, 16), 16)
        return pair("qy", low, b["q_v"].at[:, :, rows, :], b["qy"].at[low], at_offset(0, dy, dc))

    def my_copy(low):
        return pair("my", low, b["mb"], b["my"].at[low], at_offset(0, *place(low)[1:]))

    def qz_copy(dz):
        return pair("qz", dz, b["zb"].at[dz], b["qx0"].at[pl.ds(dz * 8, 8)], at_offset(dz, 0, 0))

    def mz_copy(dz):
        return pair("mz", dz, b["mz"].at[dz], b["mx0"].at[dz], at_offset(dz, 0, 0))

    for branch in range(2):
        b["mb"][branch] = jnp.full((1, 128), slots[branch], jnp.int32)
    pl.semaphore_wait(barrier, len(partners))
    for low in range(1, 8):
        my_copy(low).start()
    load_q.wait()
    for low in range(1, 8):
        qy_copy(low).start()
    head = y * 2 + c
    b["qy"][0] = b["q_v"][:, :, pl.ds(pl.multiple_of(head * 16, 16), 16), :]
    b["my"][0] = b["mb"][...]

    def build_meta(dz):
        group = lax.rem(z + dz, 4)
        for low in range(8):
            first, second = b["my"][low, 0], b["my"][low, 1]
            b["mz" if dz else "mx0"][dz, low] = jnp.where((second // 4) == group, second, first) % 4

    def build(dz):
        group = lax.rem(z + dz, 4)
        target = b["zb"] if dz else b["qx0"]
        for low in range(8):
            pick = (b["my"][low, 1] // 4) == group
            pick_rows = jnp.broadcast_to(pick, (ROWS, HD))
            rows = [b["qy"][low, branch].reshape(ROWS, HD).astype(F32) for branch in range(2)]
            chosen = jnp.where(pick_rows, rows[1], rows[0]).astype(BF)
            if dz == 0:
                target[low] = chosen
            else:
                target[dz, low] = chosen

    def x_copy(dz, side):
        batch, base = beside(side, dz)
        source = b["qx0"].at[pl.ds(dz * 8, 8)]
        return pair("x", (side, dz), source, b["qx%d" % batch].at[pl.ds(base, 8)], at_x(1 - 2 * side))

    def xm_copy(side):
        return pair("xm", side, b["mx0"], b["mx%d" % (1 + side)], at_x(1 - 2 * side))

    def f_copy(dz, side):
        batch, base = beside(side, dz)
        source = b["qx%d" % batch].at[pl.ds(base + side * 4, 4)]
        return pair("f", (side, dz), source, b["qx3"].at[pl.ds(dz * 8 + side * 4, 4)], at_x(1 - 2 * side))

    def fm_copy():
        return pair("fm", 0, b["mx1"], b["mx3"], at_x(1))

    def pass_x(dz):
        if dz:
            qz_copy(dz).wait_recv()
        for side in range(2):
            x_copy(dz, side).start()

    def pass_on(dz):
        for side in range(2):
            x_copy(dz, side).wait_recv()
            f_copy(dz, side).start()

    for slot in range(4):
        b["va"][slot, :, HD:] = jnp.ones((1024, HD), BF)
    load_k.wait()
    for slot in range(4):
        b["kt"][slot] = b["pk_v"][slot].T
    for low in range(1, 8):
        my_copy(low).wait_recv()
    for dz in range(4):
        build_meta(dz)
        if dz:
            mz_copy(dz).start()
    for low in range(1, 8):
        qy_copy(low).wait_recv()
    build(0)
    pass_x(0)
    for dz in (1, 3):
        build(dz)
        qz_copy(dz).start()
    for copy in load_own:
        copy.wait()
    own_spread(0, b)
    build(2)
    for dz in range(1, 4):
        mz_copy(dz).wait_recv()
    for side in range(2):
        xm_copy(side).start()
    qz_copy(2).start()
    own_heads(0, b, length_ref[0], (0, 2))
    for side in range(2):
        xm_copy(side).wait_recv()
    fm_copy().start()
    pass_x(1)
    pass_x(3)
    own_spread(1, b)
    own_heads(1, b, length_ref[1], (0, 2))
    fm_copy().wait_recv()
    order_places(
        [
            [(b["mx0"], dz) for dz in range(4)],
            [(b["mx%d" % (1 + side)], dz) for side in range(2) for dz in (0, 1)],
            [(b["mx%d" % (1 + side)], dz) for side in range(2) for dz in (3, 2)],
            [(b["mx3"], dz) for dz in range(4)],
        ],
        b["my"], b["order_v"], b["order_s"], b["local_sem"].at[7],
    )
    load_v.wait()
    pass_x(2)
    pass_on(0)

    def chunk(number):
        attend_chunk(
            b["qx%d" % number], (b["order_s"], number), b["kt"], b["va"], b["ot%d" % number], b["lt%d" % number]
        )

    def part_of(number, index):
        return pick_rows((b["order_s"], number), b["ot%d" % number], b["lt%d" % number], index)

    chunk(0)
    pass_on(1)

    def a_copies(side, late):
        device = at_x(-1 if side == 0 else 1)
        part = pl.ds(late * 8, 8)
        lpart = pl.ds(late * 16, 16)
        return (
            pair("a", (side, late), b["a_out"].at[side, part], b["a_in"].at[side, part], device),
            pair("al", (side, late), b["al_out"].at[side, lpart], b["al_in"].at[side, lpart], device),
        )

    def c_copies(side, dz):
        device = at_x(-1 if side == 0 else 1)
        part = pl.ds(dz * 4, 4)
        lpart = pl.ds(dz * 8, 8)
        return (
            remote(
                b["c_out"].at[side, part], b["c_in"].at[side, part], b["c_send"].at[side, dz], b["c_recv"].at[side, dz], device
            ),
            remote(
                b["cl_out"].at[side, lpart], b["cl_in"].at[side, lpart], b["cl_send"].at[side, dz], b["cl_recv"].at[side, dz],
                device,
            ),
        )

    def b_copies(side, dz):
        device = at_x(-1 if side == 0 else 1)
        part = pl.ds(dz * 4, 4)
        lpart = pl.ds(dz * 8, 8)
        return (
            remote(
                b["b_out"].at[side, part], b["b_in"].at[side, part], b["b_send"].at[side, dz], b["b_recv"].at[side, dz], device
            ),
            remote(
                b["bl_out"].at[side, lpart], b["bl_in"].at[side, lpart], b["bl_send"].at[side, dz], b["bl_recv"].at[side, dz],
                device,
            ),
        )

    def put_plain(number, base, out, lse, side, dz):
        def step(low, carry):
            rows, column = part_of(number, base + low)
            out[side, dz * 4 + low] = rows
            lse[side, pl.ds(dz * 8 + low, 1)] = to_row(column)
            return carry

        lax.fori_loop(0, 4, step, 0, unroll=4)

    for late in range(2):
        chunk(1 + late)
        for side in range(2):
            for dz in (2 * late, 2 * late + 1):
                batch, base = beside(side, dz)
                put_plain(batch, base + 4 - 4 * side, b["a_out"], b["al_out"], side, dz)
            for copy in a_copies(side, late):
                copy.start()
        if not late:
            pass_on(3)
            pass_on(2)
    for dz in DZ_ORDER:
        for side in range(2):
            f_copy(dz, side).wait_recv()
    chunk(3)
    for dz in BACK_ORDER:
        for side in range(2):
            put_plain(3, dz * 8 + side * 4, b["c_out"], b["cl_out"], side, dz)
            for copy in c_copies(side, dz):
                copy.start()

    for dz in BACK_ORDER:
        for side in range(2):
            for copy in c_copies(side, dz):
                copy.wait_recv()

            def step(low, carry):
                batch, base = beside(side, dz)
                rows, column = part_of(batch, base + side * 4 + low)
                far = to_column(b["cl_in"][side, pl.ds(dz * 8 + low, 1)])
                out, lse = merge([(rows.astype(F32), column), (b["c_in"][side, dz * 4 + low].astype(F32), far)])
                b["b_out"][side, dz * 4 + low] = out.astype(BF)
                b["bl_out"][side, pl.ds(dz * 8 + low, 1)] = to_row(lse)
                return carry

            lax.fori_loop(0, 4, step, 0, unroll=4)
            for copy in b_copies(side, dz):
                copy.start()

    def hz_copy(dz):
        part = pl.ds(dz * 8, 8)
        return pair("hz", dz, b["h_out"].at[part], b["h_in"].at[part], at_offset(dz, 0, 0, sign=-1))

    def lz_copy(dz):
        return pair("lz", dz, b["l_out"].at[dz], b["l_in"].at[dz], at_offset(dz, 0, 0, sign=-1))

    def hy_copy(low):
        return pair("hy", low, b["yb"].at[low], b["home"].at[low], at_offset(0, *place(low)[1:], sign=-1))

    def ly_copy(low):
        return pair("ly", low, b["lyb"].at[low], b["lhome"].at[low], at_offset(0, *place(low)[1:], sign=-1))

    for side in range(2):
        for copy in a_copies(side, 0) + a_copies(side, 1):
            copy.wait_recv()
    for dz in BACK_ORDER:
        for half in range(2):
            for copy in b_copies(half, dz):
                copy.wait_recv()

            def step(low, carry):
                index = dz * 8 + half * 4 + low
                rows, column = part_of(0, index)
                plain = to_column(b["al_in"][1 - half, pl.ds(dz * 8 + low, 1)])
                joined = to_column(b["bl_in"][half, pl.ds(dz * 8 + low, 1)])
                out, lse = merge(
                    [
                        (rows.astype(F32), column),
                        (b["a_in"][1 - half, dz * 4 + low].astype(F32), plain),
                        (b["b_in"][half, dz * 4 + low].astype(F32), joined),
                    ]
                )
                b["h_out" if dz else "h_in"][index] = out.astype(BF)
                b["l_out" if dz else "l_in"][dz, half * 4 + low] = to_row(lse)
                return carry

            lax.fori_loop(0, 4, step, 0, unroll=4)
        if dz:
            hz_copy(dz).start()
            lz_copy(dz).start()
    for dz in range(1, 4):
        hz_copy(dz).wait_recv()
        lz_copy(dz).wait_recv()
    for low in (4, 5, 6, 7, 2, 3, 1, 0):
        target, ltarget = ("yb", "lyb") if low else ("home", "lhome")
        for branch in range(2):
            slot = jnp.clip(b["order_s"][32 + 2 * low + branch, 0], 0, 15)
            away = lax.rem(slot // 4 - z + 4, 4)
            b[target][low, branch] = b["h_in"][away * 8 + low]
            b[ltarget][low, branch] = b["l_in"][away, low]
        if low:
            hy_copy(low).start()
            ly_copy(low).start()
    for low in range(1, 8):
        hy_copy(low).wait_recv()
        ly_copy(low).wait_recv()

    for branch in range(2):
        def step(low, carry):
            dy = low // 2
            dc = low % 2
            head = lax.rem(y + dy, 4) * 2 + lax.rem(c + dc, 2)
            lse = to_column(b["lhome"][low, branch])
            out, _ = merge(
                [(b["home"][low, branch].astype(F32), lse), (b["own_o"][branch, head], b["own_l"][branch, head])]
            )
            o_ref[branch, :, pl.ds(pl.multiple_of(head * 16, 16), 16), :] = out.astype(BF).reshape(4, 16, HD)
            return carry

        lax.fori_loop(0, 8, step, 0, unroll=4)

    for dz in range(1, 4):
        for copy in (qz_copy, mz_copy, hz_copy, lz_copy):
            copy(dz).wait_send()
    for low in range(1, 8):
        for copy in (qy_copy, my_copy, hy_copy, ly_copy):
            copy(low).wait_send()
    fm_copy().wait_send()
    for side in range(2):
        xm_copy(side).wait_send()
        for copy in a_copies(side, 0) + a_copies(side, 1):
            copy.wait_send()
        for dz in range(4):
            for copy in (x_copy(dz, side), f_copy(dz, side)) + c_copies(side, dz) + b_copies(side, dz):
                copy.wait_send()


def scratch_shapes():
    dma = pltpu.SemaphoreType.DMA
    vmem = pltpu.VMEM
    shapes = {
        "q_v": vmem((2, 4, 128, HD), BF),
        "pk_v": vmem((4, 1024, HD), BF),
        "kt": vmem((4, HD, 1024), BF),
        "va": vmem((4, 1024, 2 * HD), BF),
        "sk_v": vmem((2, 512, 8, HD), BF),
        "sv_v": vmem((2, 512, 8, HD), BF),
        "nk_v": vmem((2, 4, 8, HD), BF),
        "nv_v": vmem((2, 4, 8, HD), BF),
        "wide_k": vmem((4104, HD), F32),
        "wide_v": vmem((4104, HD), F32),
        "wide_nk": vmem((40, HD), F32),
        "wide_nv": vmem((40, HD), F32),
        "own_o": vmem((2, 8, ROWS, HD), F32),
        "own_l": vmem((2, 8, ROWS, HD), F32),
        "qy": vmem((8, 2, 4, 16, HD), BF),
        "zb": vmem((4, 8, ROWS, HD), BF),
        "mb": vmem((2, 1, 128), jnp.int32),
        "my": vmem((8, 2, 1, 128), jnp.int32),
        "mz": vmem((4, 8, 1, 128), jnp.int32),
        "order_v": vmem((48, 128), jnp.int32),
        "order_s": pltpu.SMEM((48, 128), jnp.int32),
        "l_out": vmem((4, 8, 1, 128), F32),
        "l_in": vmem((4, 8, 1, 128), F32),
        "yb": vmem((8, 2, ROWS, HD), BF),
        "home": vmem((8, 2, ROWS, HD), BF),
        "lyb": vmem((8, 2, 1, 128), F32),
        "lhome": vmem((8, 2, 1, 128), F32),
        "a_out": vmem((2, 16, ROWS, HD), BF),
        "a_in": vmem((2, 16, ROWS, HD), BF),
        "c_out": vmem((2, 16, ROWS, HD), BF),
        "c_in": vmem((2, 16, ROWS, HD), BF),
        "b_out": vmem((2, 16, ROWS, HD), BF),
        "b_in": vmem((2, 16, ROWS, HD), BF),
        "h_out": vmem((SLOTS, ROWS, HD), BF),
        "h_in": vmem((SLOTS, ROWS, HD), BF),
        "local_sem": dma((8,)),
    }
    for name in ("al", "cl", "bl"):
        shapes[name + "_out"] = vmem((2, 32, 128), F32)
        shapes[name + "_in"] = vmem((2, 32, 128), F32)
    for number in range(4):
        shapes["qx%d" % number] = vmem((SLOTS, ROWS, HD), BF)
        shapes["mx%d" % number] = vmem((4, 8, 1, 128), jnp.int32)
        shapes["ot%d" % number] = vmem((2 * TILES, ROWS, HD), BF)
        shapes["lt%d" % number] = vmem((2 * TILES, ROWS, HD), F32)
    for name, count in (
        ("qz", (4,)), ("mz", (4,)), ("qy", (8,)), ("my", (8,)), ("x", (2, 4)), ("xm", (2,)), ("f", (2, 4)),
        ("fm", (1,)), ("a", (2, 2)), ("al", (2, 2)), ("c", (2, 4)), ("cl", (2, 4)), ("b", (2, 4)), ("bl", (2, 4)),
        ("hy", (8,)), ("ly", (8,)), ("hz", (4,)), ("lz", (4,)),
    ):
        shapes[name + "_send"] = dma(count)
        shapes[name + "_recv"] = dma(count)
    return shapes


NAMES = tuple(scratch_shapes())


def body(
    queries, prefix_keys, prefix_values, suffix_keys, suffix_values, new_keys, new_values, suffix_lengths, branch_prefix,
    prefix_slot,
):
    smem = pl.BlockSpec(memory_space=pltpu.SMEM)
    hbm = pl.BlockSpec(memory_space=pl.ANY)
    return pl.pallas_call(
        kernel,
        out_shape=jax.ShapeDtypeStruct(queries.shape, BF),
        in_specs=[smem] * 3 + [hbm] * 7,
        out_specs=pl.BlockSpec(memory_space=pltpu.VMEM),
        scratch_shapes=list(scratch_shapes().values()),
        compiler_params=pltpu.CompilerParams(collective_id=0, has_side_effects=True, vmem_limit_bytes=60 << 20),
        name="attend",
    )(
        branch_prefix, prefix_slot, suffix_lengths, queries, prefix_keys[:, 0], prefix_values[:, 0], suffix_keys,
        suffix_values, new_keys, new_values,
    )


def solution(mesh):
    both = P(("grp", "shard"), None, None, None)
    prefix = P("grp", "shard", None, None)
    flat = P(("grp", "shard"))
    return jax.shard_map(
        body,
        mesh=mesh,
        in_specs=(both, prefix, prefix, both, both, both, both, flat, flat, P()),
        out_specs=both,
        check_vma=False,
    )
```

time: 71.3 us -> 69.6 us (0.976)
  Pallas kernels: 69.5 us -> 67.8 us
    pallas_call x1, Pallas kernels: 69.5 us -> 67.8 us  [body(): pl.pallas_call(kernel, out_shape=jax.ShapeDtypeStruct(queries.shape, BF),...]
where the time goes in v2:
time: 69.6 us; the launch traced here: 69.5 us
  Pallas kernels  67.8 us (97%)
  local copies, waits for them, and re-layouts  1.67 us (2%)
    pallas_call x1, Pallas kernels, body(): pl.pallas_call(kernel, out_shape=jax.ShapeDtypeStruct(queries.shape, BF),...  67.8 us
    unnamed x1, local copies, waits for them, and re-layouts  1.67 us

profile of v2, /device:TPU:1, one launch (start us, length us, event | category | flops | bytes accessed | tf_op | source)
XLA Modules:
  0.0 69.5 jit_solution(12071687161661752153)
XLA Ops:
  0.0 67.8 %attend.1 = bf16[2,4,128,128]{3,2,1,0:T(8,128)(2,1)} custom-call(s32[2]{0:T(128)} %prefix_ref.1, s32[16]{0:T(128)} %slot_ref.1, s32[2]{0:T(128)} %length_ref.1, bf16[2,4,128,128]{3,2,1,0:T(8,128)(2,1)} %q_hbm.1, bf16[4,1024,128]{2,1,0:T(8,128)(2,1)} %bitcast.2, bf16[4,1024,128]{2,1,0:T(8,128)(2,1)} %bitcast.3, bf16[2,512,8,128]{3,2,1,0:T(8,128)(2,1)} %sk_hbm.1, ...), custom_call_target="tpu_custom_call" | custom-call | tf_op jit(solution)/shard_map/attend/pallas_call | solution.py:601
  67.8 1.7 %copy.12 = bf16[2,4,128,128]{3,2,1,0:T(8,128)(2,1)} copy(bf16[2,4,128,128]{3,2,1,0:T(8,128)(2,1)} %attend.1) | data formatting | bytes 524288

commit v3 on v2

--- a/solution.py
+++ b/solution.py
@@ -16,7 +16,7 @@
 ROWS = 64
 SLOTS = 32
 TILES = 18
-GROUP = 6
+GROUP = 9
 DZ_ORDER = (0, 1, 3, 2)
 BACK_ORDER = (2, 1, 3, 0)
 SCALE = math.log2(math.e) / math.sqrt(HD)
@@ -245,7 +245,7 @@
     for low in range(1, 8):
         my_copy(low).start()
     load_q.wait()
-    for low in range(1, 8):
+    for low in (4, 5, 2, 3, 6, 7, 1):
         qy_copy(low).start()
     head = y * 2 + c
     b["qy"][0] = b["q_v"][:, :, pl.ds(pl.multiple_of(head * 16, 16), 16), :]
@@ -302,6 +302,10 @@
     load_k.wait()
     for slot in range(4):
         b["kt"][slot] = b["pk_v"][slot].T
+    for copy in load_own:
+        copy.wait()
+    own_spread(0, b)
+    own_heads(0, b, length_ref[0], (0, 2))
     for low in range(1, 8):
         my_copy(low).wait_recv()
     for dz in range(4):
@@ -315,23 +319,19 @@
     for dz in (1, 3):
         build(dz)
         qz_copy(dz).start()
-    for copy in load_own:
-        copy.wait()
-    own_spread(0, b)
+    own_spread(1, b)
     build(2)
     for dz in range(1, 4):
         mz_copy(dz).wait_recv()
     for side in range(2):
         xm_copy(side).start()
     qz_copy(2).start()
-    own_heads(0, b, length_ref[0], (0, 2))
+    own_heads(1, b, length_ref[1], (0, 2))
     for side in range(2):
         xm_copy(side).wait_recv()
     fm_copy().start()
     pass_x(1)
     pass_x(3)
-    own_spread(1, b)
-    own_heads(1, b, length_ref[1], (0, 2))
     fm_copy().wait_recv()
     order_places(
         [
@@ -356,6 +356,8 @@
 
     chunk(0)
     pass_on(1)
+    pass_on(3)
+    pass_on(2)
 
     def a_copies(side, late):
         device = at_x(-1 if side == 0 else 1)
@@ -403,7 +405,7 @@
 
         lax.fori_loop(0, 4, step, 0, unroll=4)
 
-    for late in range(2):
+    def near_chunk(late):
         chunk(1 + late)
         for side in range(2):
             for dz in (2 * late, 2 * late + 1):
@@ -411,9 +413,8 @@
                 put_plain(batch, base + 4 - 4 * side, b["a_out"], b["al_out"], side, dz)
             for copy in a_copies(side, late):
                 copy.start()
-        if not late:
-            pass_on(3)
-            pass_on(2)
+
+    near_chunk(0)
     for dz in DZ_ORDER:
         for side in range(2):
             f_copy(dz, side).wait_recv()
@@ -423,6 +424,7 @@
             put_plain(3, dz * 8 + side * 4, b["c_out"], b["cl_out"], side, dz)
             for copy in c_copies(side, dz):
                 copy.start()
+    near_chunk(1)
 
     for dz in BACK_ORDER:
         for side in range(2):

time: 69.6 us -> 69.4 us (level)
  no operation moved by 1% of the time
where the time goes in v3:
time: 69.4 us; the launch traced here: 69.2 us
  Pallas kernels  67.6 us (97%)
  local copies, waits for them, and re-layouts  1.67 us (2%)
    pallas_call x1, Pallas kernels, body(): pl.pallas_call(kernel, out_shape=jax.ShapeDtypeStruct(queries.shape, BF),...  67.6 us
    unnamed x1, local copies, waits for them, and re-layouts  1.67 us

profile of v3, /device:TPU:1, one launch (start us, length us, event | category | flops | bytes accessed | tf_op | source)
XLA Modules:
  0.0 69.2 jit_solution(3069981181071353845)
XLA Ops:
  0.0 67.6 %attend.1 = bf16[2,4,128,128]{3,2,1,0:T(8,128)(2,1)} custom-call(s32[2]{0:T(128)} %prefix_ref.1, s32[16]{0:T(128)} %slot_ref.1, s32[2]{0:T(128)} %length_ref.1, bf16[2,4,128,128]{3,2,1,0:T(8,128)(2,1)} %q_hbm.1, bf16[4,1024,128]{2,1,0:T(8,128)(2,1)} %bitcast.2, bf16[4,1024,128]{2,1,0:T(8,128)(2,1)} %bitcast.3, bf16[2,512,8,128]{3,2,1,0:T(8,128)(2,1)} %sk_hbm.1, ...), custom_call_target="tpu_custom_call" | custom-call | tf_op jit(solution)/shard_map/attend/pallas_call | solution.py:603
  67.6 1.7 %copy.12 = bf16[2,4,128,128]{3,2,1,0:T(8,128)(2,1)} copy(bf16[2,4,128,128]{3,2,1,0:T(8,128)(2,1)} %attend.1) | data formatting | bytes 524288
